TPU v7x, 256 devices: a whole 4x4x8 slice. The times are simulated.
256 devices in a mesh: segment: 2 (over core), dom: 32 (over x, z), rep: 4 (over y).
Axes of the slice: x: 4, y: 4, z: 8, core: 2. Of those that a mesh axis runs over, the one named last changes fastest.
Arguments:
- features: bfloat16 [4, 2, 8192, 512], P('rep', None, 'dom'), may hold values from -6 to 6
- tile_vals: bfloat16 [4, 2, 192, 128, 128], P('rep', None, 'dom'), may hold values from -0.3125 to 0.3125
- tile_cols: int32 [4, 2, 192], P('rep', None, 'dom'), may hold values from 0 to 3, as said below
- send_lists: int32 [4, 2, 64, 1], P('rep', None, 'dom'), may hold values from 0 to 1
- section_layers: int32 [2], replicated, may hold values from 1 to 2, as said below
- weights: bfloat16 [4, 512, 512], P('segment'), may hold values from -0.25 to 0.25
- cotangent: bfloat16 [4, 2, 8192, 512], P('rep', None, 'dom'), may hold values from -0.1875 to 0.1875
Outputs:
- weight_grads: float32 [4, 512, 512], P('segment')
Inputs may be any that keep to these rules, and one draw needn't show every extreme that they name: `tile_cols`: in each row block's group of 3 tiles the first names the row block itself, the second a received block, and every received block of a partition is named by some second tile; the rest name any block. `section_layers`: one section has exactly 2 layers.
All inputs are finite; a program needn't handle non-finite values.
Results may differ from a plain program's by a relative error of at most 0.02.
Values may be sent and summed in bfloat16 or wider, within the bound.
No kernel may reach another device: no remote copies, remote signals or barrier semaphores. Data moves between devices by JAX's collectives and lax.ppermute only.
A program may use at most 64 MiB of HBM per device.

v0:
```python
import functools
import math

import jax
import jax.numpy as jnp
import numpy as np
from jax import lax
from jax.experimental import pallas as pl
from jax.experimental.pallas import tpu as pltpu
from jax.sharding import Mesh
from jax.sharding import PartitionSpec as P

BLOCK = 128
ROWS = 256
FEAT = 512
KEEP = 0.9
RESTART = 0.1
STRENGTH = 0.5
C0 = math.sqrt(2.0 / math.pi)
C1 = 0.044715
BF = jnp.bfloat16
F32 = jnp.float32
DOM = ("x", "z")
PLANE = ("x", "rep")


def beta(k):
    return float(np.log(np.float32(STRENGTH / k + 1.0)))


def spec(shape, dtype):
    return jax.ShapeDtypeStruct(shape, dtype)


def call(kernel, outs, scalars, arrays, name, space=pltpu.VMEM, scratch=(), aliases=None):
    smem = [pl.BlockSpec(memory_space=pltpu.SMEM)] * len(scalars)
    held = [pl.BlockSpec(memory_space=space)] * len(arrays)
    if space is pltpu.HBM:
        arrays = [pltpu.with_memory_space_constraint(a, space) for a in arrays]
    return pl.pallas_call(
        kernel,
        out_shape=outs,
        in_specs=smem + held,
        scratch_shapes=list(scratch),
        input_output_aliases=aliases or {},
        out_specs=jax.tree.map(lambda _: pl.BlockSpec(memory_space=pltpu.VMEM), outs),
        compiler_params=pltpu.CompilerParams(vmem_limit_bytes=12 * 1024 * 1024),
        name=name,
    )(*scalars, *arrays)


def mm(a, b):
    return jnp.dot(a, b, preferred_element_type=F32)


def mm_nt(a, b):
    return lax.dot_general(a, b, (((1,), (1,)), ((), ())), preferred_element_type=F32)


def mm_tn(a, b):
    return lax.dot_general(a, b, (((0,), (0,)), ((), ())), preferred_element_type=F32)


N_FLAGS = 16


def first_kernel(
    micro, sends, cols, tiles_all, feats, cot, to_left, to_right, tiles, feats_own, cot_own, flags, sends_in, cols_in, sems
):
    m = micro[0]
    copies = [
        pltpu.make_async_copy(sends, sends_in, sems.at[0]),
        pltpu.make_async_copy(cols, cols_in, sems.at[1]),
        pltpu.make_async_copy(feats.at[m], feats_own, sems.at[2]),
        pltpu.make_async_copy(tiles_all.at[m], tiles, sems.at[3]),
        pltpu.make_async_copy(cot.at[m], cot_own, sems.at[4]),
    ]
    for copy in copies:
        copy.start()
    copies[0].wait()
    copies[1].wait()

    def put(row, value):
        flags[row : row + 1, :] = jnp.full((1, FEAT), value.astype(F32), F32)

    put(0, sends_in[m, 0])
    put(1, sends_in[m, 1])
    for b in range(2):
        for s in range(2):
            row = 2 * b + s
            put(2 + row, jnp.where(cols_in[m, 3 * b + 1] == 2 + s, 1, 0))
            put(6 + row, jnp.where(cols_in[m, 3 * b + 2] == 2 + s, 1, 0))
            put(10 + row, jnp.where(cols_in[m, 3 * b + 2] == s, 1, 0))
    copies[2].wait()
    to_left[...] = feats_own[sends_in[m, 0]]
    to_right[...] = feats_own[sends_in[m, 1]]
    copies[3].wait()
    copies[4].wait()


def choose(use_own, row, mine, other, out):
    @pl.when(use_own)
    def _():
        out[...] = mine[row]

    @pl.when(jnp.logical_not(use_own))
    def _():
        out[...] = other[row]


def squares(tiles, flags, rem, own):
    zero = jnp.zeros((BLOCK, BLOCK), BF)
    for b in range(2):
        rows = pl.ds(b * BLOCK, BLOCK)
        first, second, third = (tiles[3 * b + i].astype(F32) for i in range(3))
        for s in range(2):
            span = pl.ds(s * BLOCK, BLOCK)
            at = (rows, span)
            hit1, hit2, hit3 = (flags[r : r + 1, :BLOCK] for r in (2 + 2 * b + s, 6 + 2 * b + s, 10 + 2 * b + s))
            rem[(0, *at)] = (second * hit1).astype(BF)
            rem[(1, *at)] = (third * hit2).astype(BF)
            own[(0, *at)] = first.astype(BF) if s == b else zero
            own[(1, *at)] = (third * hit3).astype(BF)


def prep_kernel(micro, tiles, flags, feats, weights, other, rem, own, base, w1):
    squares(tiles, flags, rem, own)
    h = feats[...].reshape(ROWS, FEAT)
    base[...] = KEEP * (mm(own[0], h) + mm(own[1], h)) + RESTART * h.astype(F32)
    choose(micro[0] == 0, 0, weights, other, w1)


def mixed(base, from_left, from_right, rem):
    recv = jnp.concatenate([from_left[...], from_right[...]], axis=0)
    return (base[...] + KEEP * (mm(rem[0], recv) + mm(rem[1], recv))).astype(BF)


def gelu_parts(value):
    return jnp.tanh(C0 * (value + C1 * (value * value * value)))


def gelu_slope(value):
    t = gelu_parts(value)
    return 0.5 * (1.0 + t) + (0.5 * C0) * value * (1.0 - t * t) * (1.0 + (3.0 * C1) * (value * value))


def pick(flags, entry, value):
    return jnp.where(flags[entry : entry + 1, :] > 0.5, value[BLOCK:], value[:BLOCK])


def forward_kernel(k, flags, base, from_left, from_right, rem, weight, out, mix, hidden, to_left, to_right):
    p = mixed(base, from_left, from_right, rem)
    mix[...] = p
    z = (1.0 - beta(k)) * p.astype(F32) + beta(k) * mm(p, weight[...])
    hidden[...] = z
    h = 0.5 * z * (1.0 + gelu_parts(z))
    out[...] = h.astype(BF)
    to_left[...] = pick(flags, 0, h).astype(BF)
    to_right[...] = pick(flags, 1, h).astype(BF)


def rest_kernel(out, feats, own, hidden, base, slope):
    h = out[...]
    local = mm(own[0], h) + mm(own[1], h)
    base[...] = KEEP * local + RESTART * feats[...].reshape(ROWS, FEAT).astype(F32)
    slope[...] = gelu_slope(hidden[...])


def rest1_kernel(
    micro, layers, out, feats, own, hidden, weights, other, base, slope, w2
):
    rest_kernel(out, feats, own, hidden, base, slope)
    two_first = layers[0] == 2
    choose(two_first == (micro[0] == 0), jnp.where(two_first, 1, 0), weights, other, w2)


def rest2_kernel(micro, layers, out, feats, own, hidden, weights, other, base, slope, w3, w4):
    rest_kernel(out, feats, own, hidden, base, slope)
    use_own = micro[0] == 1
    choose(use_own, jnp.where(layers[0] == 2, 0, 1), weights, other, w3)
    choose(use_own, 1, weights, other, w4)


def send_back(k, gz, weight, rem, gz_round, ga, to_left, to_right):
    gzb = gz.astype(BF)
    gz_round[...] = gzb
    gp = (1.0 - beta(k)) * gz + beta(k) * mm_nt(gzb, weight[...])
    g = (KEEP * gp).astype(BF)
    ga[...] = g
    gb = (mm_tn(rem[0], g) + mm_tn(rem[1], g)).astype(BF)
    to_left[...] = gb[:BLOCK]
    to_right[...] = gb[BLOCK:]


def top_kernel(
    k, base, from_left, from_right, rem, weight, cot, mix, gz_round, ga, to_left, to_right, *unwritten
):
    p = mixed(base, from_left, from_right, rem)
    mix[...] = p
    z = (1.0 - beta(k)) * p.astype(F32) + beta(k) * mm(p, weight[...])
    gz = cot[...].reshape(ROWS, FEAT).astype(F32) * gelu_slope(z)
    send_back(k, gz, weight, rem, gz_round, ga, to_left, to_right)


def gathered(flags, own_grad, from_left, from_right):
    left = from_left[...].astype(F32)
    right = from_right[...].astype(F32)
    hit_left, hit_right = flags[0:1, :], flags[1:2, :]
    low = own_grad[:BLOCK] + (1.0 - hit_left) * left + (1.0 - hit_right) * right
    high = own_grad[BLOCK:] + hit_left * left + hit_right * right
    return jnp.concatenate([low, high], axis=0)


def backward_kernel(k, flags, own_grad, from_left, from_right, slope, weight, rem, gz_round, ga, to_left, to_right):
    gz = gathered(flags, own_grad, from_left, from_right) * slope[...]
    send_back(k, gz, weight, rem, gz_round, ga, to_left, to_right)


def backward_rest_kernel(k, ga, own, mix, gz_round, own_grad, weight_grad):
    g = ga[...]
    own_grad[...] = mm_tn(own[0], g) + mm_tn(own[1], g)
    weight_grad[...] = (beta(k) * mm_tn(mix[...], gz_round[...])).astype(BF)


def slots_kernel(micro, layers, ga, own, mix, gz_round, grad3, grad4, own_grad, kept, given):
    g = ga[...]
    own_grad[...] = mm_tn(own[0], g) + mm_tn(own[1], g)
    grad2 = (beta(2) * mm_tn(mix[...], gz_round[...])).astype(BF)
    none = jnp.zeros((FEAT, FEAT), BF)
    two_first = layers[0] == 2
    four = two_first & (layers[1] == 2)

    def fill(low, high):
        @pl.when(two_first)
        def _():
            low[1] = grad2
            high[0] = grad3[...]

        @pl.when(jnp.logical_not(two_first))
        def _():
            low[1] = none
            high[0] = grad2
            high[1] = grad3[...]

        @pl.when(four)
        def _():
            high[1] = grad4[...]

        @pl.when(two_first & jnp.logical_not(four))
        def _():
            high[1] = none

    @pl.when(micro[0] == 0)
    def _():
        fill(kept, given)

    @pl.when(micro[0] == 1)
    def _():
        fill(given, kept)


def last_kernel(micro, flags, own_grad, from_left, from_right, slope, mix, kept_in, given_in, kept, given):
    gz = gathered(flags, own_grad, from_left, from_right) * slope[...]
    grad = (beta(1) * mm_tn(mix[...], gz.astype(BF))).astype(BF)

    @pl.when(micro[0] == 0)
    def _():
        kept[0] = grad

    @pl.when(micro[0] == 1)
    def _():
        given[0] = grad


HALF = spec((BLOCK, FEAT), BF)
ROWS_BF = spec((ROWS, FEAT), BF)
PAIR = spec((2, BLOCK, FEAT), BF)
ROWS_F32 = spec((ROWS, FEAT), F32)
GRAD = spec((FEAT, FEAT), BF)
SLOTS = spec((2, FEAT, FEAT), BF)
SQUARE = spec((2, ROWS, ROWS), BF)
BACK = (ROWS_BF, ROWS_BF, HALF, HALF)


def exchange(to_left, to_right):
    count = lax.axis_size("x") * lax.axis_size("z")
    up = [(i, (i + 1) % count) for i in range(count)]
    down = [((i + 1) % count, i) for i in range(count)]
    return lax.ppermute(to_right, DOM, up), lax.ppermute(to_left, DOM, down)


def forward(k, flags, base, recv, rem, weight):
    outs = (ROWS_BF, ROWS_BF, ROWS_F32, HALF, HALF)
    out, mix, hidden, left, right = call(
        functools.partial(forward_kernel, k), outs, [], [flags, base, *recv, rem, weight], f"forward{k}"
    )
    return out, mix, hidden, exchange(left, right)


def top(k, base, recv, rem, weight, cot, more=()):
    return call(
        functools.partial(top_kernel, k),
        (ROWS_BF, *BACK, *more),
        [],
        [base, *recv, rem, weight, cot],
        f"top{k}",
    )


def back_rest(k, ga, own, mix, gz_round):
    return call(
        functools.partial(backward_rest_kernel, k),
        (ROWS_F32, GRAD),
        [],
        [ga, own, mix, gz_round],
        f"backrest{k}",
    )


def back(k, flags, own_grad, recv, slope, weight, rem):
    return call(
        functools.partial(backward_kernel, k),
        BACK,
        [],
        [flags, own_grad, *recv, slope, weight, rem],
        f"back{k}",
    )


def along_z(piece):
    depth = lax.axis_size("z")
    got = lax.ppermute(piece, "z", [(i, depth - 1 - i) for i in range(depth)])
    piece = (piece.astype(F32) + got.astype(F32)).astype(BF)
    near, far, both = (
        lax.ppermute(piece, "z", [(i, i ^ k) for i in range(depth)]).astype(F32) for k in (1, 2, 3)
    )
    return ((piece.astype(F32) + near) + (far + both)).astype(BF)


def shards(features, tile_vals, tile_cols, send_lists, section_layers, weights, cotangent):
    micro = jnp.full((1,), lax.axis_index("segment"), jnp.int32)
    layers = section_layers
    left, right, tiles, feats, cot, flags = call(
        first_kernel,
        (HALF, HALF, spec((6, BLOCK, BLOCK), BF), PAIR, PAIR, spec((N_FLAGS, FEAT), F32)),
        [micro],
        [
            send_lists.reshape(2, 2),
            tile_cols.reshape(2, 6),
            tile_vals.reshape(2, 6, BLOCK, BLOCK),
            features.reshape(2, 2, BLOCK, FEAT),
            cotangent.reshape(2, 2, BLOCK, FEAT),
        ],
        "first",
        pltpu.HBM,
        [
            pltpu.SMEM((2, 2), jnp.int32),
            pltpu.SMEM((2, 6), jnp.int32),
            pltpu.SemaphoreType.DMA((5,)),
        ],
    )
    recv = exchange(left, right)
    weights, layers, left = lax.optimization_barrier((weights, layers, left))
    four = (layers[0] + layers[1]) == 4
    tiles, _ = lax.optimization_barrier((tiles, four.astype(jnp.int32)))
    other = lax.ppermute(weights, "segment", [(0, 1), (1, 0)])
    rem, own, base, w1 = call(
        prep_kernel,
        (SQUARE, SQUARE, ROWS_F32, GRAD),
        [micro],
        [tiles, flags, feats, weights, other],
        "prep",
    )
    out, mix1, hidden, recv = forward(1, flags, base, recv, rem, w1)
    base, slope1, w2 = call(
        rest1_kernel,
        (ROWS_F32, ROWS_F32, GRAD),
        [micro, layers],
        [out, feats, own, hidden, weights, other],
        "rest1",
    )
    out, mix2, hidden, recv = forward(2, flags, base, recv, rem, w2)
    base, slope2, w3, w4 = call(
        rest2_kernel,
        (ROWS_F32, ROWS_F32, GRAD, GRAD),
        [micro, layers],
        [out, feats, own, hidden, weights, other],
        "rest2",
    )

    def with_three(base, recv, w3, w4):
        *outs, unwritten = top(3, base, recv, rem, w3, cot, (GRAD,))
        return (unwritten, *outs)

    def with_four(base, recv, w3, w4):
        out, mix3, hidden, recv = forward(3, flags, base, recv, rem, w3)
        base, slope3 = call(
            rest_kernel, (ROWS_F32, ROWS_F32), [], [out, feats, own, hidden], "rest3"
        )
        mix4, gz, ga, left, right = top(4, base, recv, rem, w4, cot)
        recv = exchange(left, right)
        own_grad, grad4 = back_rest(4, ga, own, mix4, gz)
        return (grad4, mix3, *back(3, flags, own_grad, recv, slope3, w3, rem))

    grad4, mix3, gz, ga, left, right = lax.cond(four, with_four, with_three, base, recv, w3, w4)
    recv = exchange(left, right)
    own_grad, grad3 = back_rest(3, ga, own, mix3, gz)
    gz, ga, left, right = back(2, flags, own_grad, recv, slope2, w2, rem)
    recv = exchange(left, right)
    own_grad, kept, given = call(
        slots_kernel,
        (ROWS_F32, SLOTS, SLOTS),
        [micro, layers],
        [ga, own, mix2, gz, grad3, grad4],
        "slots",
    )
    kept, given = call(
        last_kernel,
        (SLOTS, SLOTS),
        [micro],
        [flags, own_grad, *recv, slope1, mix1, kept, given],
        "last",
        aliases={7: 0, 8: 1},
    )
    taken = lax.ppermute(given, "segment", [(0, 1), (1, 0)])
    part = (kept.astype(F32) + taken.astype(F32)).astype(BF)
    plane = lax.axis_size("x") * lax.axis_size("rep")
    pieces = lax.all_to_all(part.reshape(plane, -1, FEAT), PLANE, 0, 0, tiled=True)
    piece = along_z(jnp.sum(pieces.astype(F32), axis=0).astype(BF))
    whole = lax.all_to_all(
        jnp.broadcast_to(piece[None], (plane,) + piece.shape), PLANE, 0, 0, tiled=True
    )
    return whole.reshape(2, FEAT, FEAT).astype(F32)


def solution(mesh):
    sizes = dict(mesh.shape)
    grid = Mesh(
        mesh.devices.reshape(sizes["segment"], 4, sizes["dom"] // 4, sizes["rep"]),
        ("segment", "x", "z", "rep"),
    )
    placed = (
        P("rep", None, DOM, None),
        P("rep", None, DOM, None, None),
        P("rep", None, DOM),
        P("rep", None, DOM, None),
        P(),
        P("segment", None, None),
        P("rep", None, DOM, None),
    )
    return jax.shard_map(
        shards, mesh=grid, in_specs=placed, out_specs=P("segment", None, None), check_vma=False
    )
```

profile of v0, /device:TPU:32, one launch (start us, length us, event | category | flops | bytes accessed | tf_op | source)
XLA Modules:
  0.0 110.6 jit_solution(2875137730658263153)
XLA Ops:
  0.0 1.3 %first.1 = (bf16[128,512]{1,0:T(8,128)(2,1)S(1)}, bf16[128,512]{1,0:T(8,128)(2,1)S(1)}, bf16[6,128,128]{2,1,0:T(8,128)(2,1)S(1)}, bf16[2,128,512]{2,1,0:T(8,128)...) custom-call(s32[1]{0:T(128)} %bitcast.micro, s32[2,2]{1,0:T(2,128)} %bitcast.17, s32[2,6]{1,0:T(2,128)} %bitcast.18, ...), custom_call_target="tpu_custom_call" | custom-call | tf_op jit(solution)/shard_map/first/pallas_call | solution.py:40
  1.3 0.1 collective-permute-start.4
  1.4 2.0 %collective-permute-start.5 = (bf16[128,512]{1,0:T(8,128)(2,1)S(1)}, bf16[128,512]{1,0:T(8,128)(2,1)S(1)}, u32[]{:S(2)}, u32[]{:S(2)}) collective-permute-start(bf16[128,512]{1,0:T(8,128)(2,1)S(1)} %get-tuple-element.132), channel_id=1, source_target_pairs={{0,4},{4,8},{8,12},{12,16},{16,20},{20,24},{24,28},{28,32},{32,36}... | collective-permute-start | bytes 393224 | tf_op jit(solution)/shard_map/ppermute | solution.py:289
  3.4 0.1 collective-permute-start.6
  3.5 1.3 %fusion = (s32[1]{0:T(128)}, s32[1]{0:T(128)}) fusion(s32[2]{0:T(128)} %layers.2), kind=kLoop, calls=%fused_computation.4 | loop fusion | bytes 16 | tf_op jit(solution)/shard_map/slice | solution.py:364
  6.0 0.0 copy-start.1
  6.0 0.4 prep.1
  6.4 0.0 copy-start.2
  6.4 0.9 collective-permute-done.5.from_left
  7.4 1.7 %collective-permute-done.6.from_right = bf16[128,512]{1,0:T(8,128)(2,1)S(1)} collective-permute-done((bf16[128,512]{1,0:T(8,128)(2,1)S(1)}, bf16[128,512]{1,0:T(8,128)(2,1)S(1)}, u32[]{:S(2)}, u32[]{:S(2)}) %collective-permute-start.6) | collective-permute-done | bytes 131104 | tf_op jit(solution)/shard_map/ppermute | solution.py:289
  9.1 0.7 forward1.1
  9.8 3.2 %collective-permute-start.7 = (bf16[128,512]{1,0:T(8,128)(2,1)S(1)}, bf16[128,512]{1,0:T(8,128)(2,1)S(1)}, u32[]{:S(2)}, u32[]{:S(2)}) collective-permute-start(bf16[128,512]{1,0:T(8,128)(2,1)S(1)} %get-tuple-element.139), channel_id=1, source_target_pairs={{0,4},{4,8},{8,12},{12,16},{16,20},{20,24},{24,28},{28,32},{32,36}... | collective-permute-start | bytes 393224 | tf_op jit(solution)/shard_map/ppermute | solution.py:289
  13.0 1.6 %collective-permute-start.8 = (bf16[128,512]{1,0:T(8,128)(2,1)S(1)}, bf16[128,512]{1,0:T(8,128)(2,1)S(1)}, u32[]{:S(2)}, u32[]{:S(2)}) collective-permute-start(bf16[128,512]{1,0:T(8,128)(2,1)S(1)} %get-tuple-element.140), channel_id=1, source_target_pairs={{4,0},{8,4},{12,8},{16,12},{20,16},{24,20},{28,24},{32,28},{36,32}... | collective-permute-start | bytes 393224 | tf_op jit(solution)/shard_map/ppermute | solution.py:289
  14.6 1.4 %rest1.1 = (f32[256,512]{1,0:T(8,128)S(1)}, f32[256,512]{1,0:T(8,128)S(1)}, bf16[512,512]{1,0:T(8,128)(2,1)S(1)}) custom-call(s32[1]{0:T(128)} %bitcast.micro, s32[2]{0:T(128)S(1)} %copy-done.1, bf16[256,512]{1,0:T(8,128)(2,1)S(1)} %get-tuple-element.135.out, bf16[2,128,512]{2,1,0:T(8,128)(2,1)S(1)} %get-tuple-element.129.feats, ...), custom_call_target="tpu_custom_call" | custom-call | tf_op jit(solution)/shard_map/rest1/pallas_call | solution.py:40
  16.0 2.0 %collective-permute-done.7.from_left = bf16[128,512]{1,0:T(8,128)(2,1)S(1)} collective-permute-done((bf16[128,512]{1,0:T(8,128)(2,1)S(1)}, bf16[128,512]{1,0:T(8,128)(2,1)S(1)}, u32[]{:S(2)}, u32[]{:S(2)}) %collective-permute-start.7) | collective-permute-done | bytes 131104 | tf_op jit(solution)/shard_map/ppermute | solution.py:289
  18.0 0.9 collective-permute-done.8.from_right
  18.9 0.7 forward2.1
  19.6 2.1 %collective-permute-start.9 = (bf16[128,512]{1,0:T(8,128)(2,1)S(1)}, bf16[128,512]{1,0:T(8,128)(2,1)S(1)}, u32[]{:S(2)}, u32[]{:S(2)}) collective-permute-start(bf16[128,512]{1,0:T(8,128)(2,1)S(1)} %get-tuple-element.145), channel_id=1, source_target_pairs={{0,4},{4,8},{8,12},{12,16},{16,20},{20,24},{24,28},{28,32},{32,36}... | collective-permute-start | bytes 393224 | tf_op jit(solution)/shard_map/ppermute | solution.py:289
  21.7 2.2 %collective-permute-start.10 = (bf16[128,512]{1,0:T(8,128)(2,1)S(1)}, bf16[128,512]{1,0:T(8,128)(2,1)S(1)}, u32[]{:S(2)}, u32[]{:S(2)}) collective-permute-start(bf16[128,512]{1,0:T(8,128)(2,1)S(1)} %get-tuple-element.146), channel_id=1, source_target_pairs={{4,0},{8,4},{12,8},{16,12},{20,16},{24,20},{28,24},{32,28},{36,32}... | collective-permute-start | bytes 393224 | tf_op jit(solution)/shard_map/ppermute | solution.py:289
  23.9 1.4 %rest2.1 = (f32[256,512]{1,0:T(8,128)S(1)}, f32[256,512]{1,0:T(8,128)S(1)}, bf16[512,512]{1,0:T(8,128)(2,1)S(1)}, bf16[512,512]{1,0:T(8,128)(2,1)S(1)}) custom-call(s32[1]{0:T(128)} %bitcast.micro, s32[2]{0:T(128)S(1)} %copy-done.1, bf16[256,512]{1,0:T(8,128)(2,1)S(1)} %get-tuple-element.142.out, bf16[2,128,512]{2,1,0:T(8,128)(2,1)S(1)} %get-tuple-element.129.feats, ...), custom_call_target="tpu_custom_call" | custom-call | tf_op jit(solution)/shard_map/rest2/pallas_call | solution.py:40
  25.4 1.4 %collective-permute-done.9 = bf16[128,512]{1,0:T(8,128)(2,1)S(1)} collective-permute-done((bf16[128,512]{1,0:T(8,128)(2,1)S(1)}, bf16[128,512]{1,0:T(8,128)(2,1)S(1)}, u32[]{:S(2)}, u32[]{:S(2)}) %collective-permute-start.9) | collective-permute-done | bytes 131104 | tf_op jit(solution)/shard_map/ppermute | solution.py:289
  26.8 1.5 %conditional.1 = (bf16[512,512]{1,0:T(8,128)(2,1)S(1)}, bf16[256,512]{1,0:T(8,128)(2,1)S(1)}, bf16[256,512]{1,0:T(8,128)(2,1)S(1)}, bf16[256,512]{1,0:T(8,128)(2...) conditional(s32[]{:T(128)} %bitcast.6, (f32[256,512]{1,0:T(8,128)S(1)}, ...), branch_computations={%region_0.0_spmd, %region_1.0_spmd} | conditional | bytes 2097360 | solution.py:405
  26.8 1.3 %top3.1 = (bf16[256,512]{1,0:T(8,128)(2,1)S(1)}, bf16[256,512]{1,0:T(8,128)(2,1)S(1)}, bf16[256,512]{1,0:T(8,128)(2,1)S(1)}, bf16[128,512]{1,0:T(8,128)(2,1)S(1)...) custom-call(f32[256,512]{1,0:T(8,128)S(1)} %get-tuple-element.37.base, ...), custom_call_target="tpu_custom_call" | custom-call | tf_op jit(solution)/shard_map/cond/branch_0_fun/top3/pallas_call | solution.py:40
  28.3 1.5 %collective-permute-start.11 = (bf16[128,512]{1,0:T(8,128)(2,1)S(1)}, bf16[128,512]{1,0:T(8,128)(2,1)S(1)}, u32[]{:S(2)}, u32[]{:S(2)}) collective-permute-start(bf16[128,512]{1,0:T(8,128)(2,1)S(1)} %get-tuple-element.154), channel_id=1, source_target_pairs={{0,4},{4,8},{8,12},{12,16},{16,20},{20,24},{24,28},{28,32},{32,36}... | collective-permute-start | bytes 393224 | tf_op jit(solution)/shard_map/ppermute | solution.py:289
  29.8 4.0 %collective-permute-start.12 = (bf16[128,512]{1,0:T(8,128)(2,1)S(1)}, bf16[128,512]{1,0:T(8,128)(2,1)S(1)}, u32[]{:S(2)}, u32[]{:S(2)}) collective-permute-start(bf16[128,512]{1,0:T(8,128)(2,1)S(1)} %get-tuple-element.155), channel_id=1, source_target_pairs={{4,0},{8,4},{12,8},{16,12},{20,16},{24,20},{28,24},{32,28},{36,32}... | collective-permute-start | bytes 393224 | tf_op jit(solution)/shard_map/ppermute | solution.py:289
  33.8 1.4 %backrest3.1 = (f32[256,512]{1,0:T(8,128)S(1)}, bf16[512,512]{1,0:T(8,128)(2,1)S(1)}) custom-call(bf16[256,512]{1,0:T(8,128)(2,1)S(1)} %get-tuple-element.150.ga, bf16[2,256,256]{2,1,0:T(8,128)(2,1)} %copy-done.2, bf16[256,512]{1,0:T(8,128)(2,1)S(1)} %get-tuple-element.151.mix, bf16[256,512]{1,0:T(8,128)(2,1)S(1)} %get-tuple-element.152.gz_round), custom_call_target="tpu_custom_call" | custom-call | tf_op jit(solution)/shard_map/backrest3/pallas_call | solution.py:40
  35.2 1.4 %collective-permute-done.11.from_left = bf16[128,512]{1,0:T(8,128)(2,1)S(1)} collective-permute-done((bf16[128,512]{1,0:T(8,128)(2,1)S(1)}, bf16[128,512]{1,0:T(8,128)(2,1)S(1)}, u32[]{:S(2)}, u32[]{:S(2)}) %collective-permute-start.11) | collective-permute-done | bytes 131104 | tf_op jit(solution)/shard_map/ppermute | solution.py:289
  36.7 0.7 back2.1
  37.4 0.1 collective-permute-start.13
  37.5 5.4 %collective-permute-start.14 = (bf16[128,512]{1,0:T(8,128)(2,1)S(1)}, bf16[128,512]{1,0:T(8,128)(2,1)S(1)}, u32[]{:S(2)}, u32[]{:S(2)}) collective-permute-start(bf16[128,512]{1,0:T(8,128)(2,1)S(1)} %get-tuple-element.164), channel_id=1, source_target_pairs={{4,0},{8,4},{12,8},{16,12},{20,16},{24,20},{28,24},{32,28},{36,32}... | collective-permute-start | bytes 393224 | tf_op jit(solution)/shard_map/ppermute | solution.py:289
  42.9 1.2 %slots.1 = (f32[256,512]{1,0:T(8,128)S(1)}, bf16[2,512,512]{2,1,0:T(8,128)(2,1)S(1)}, bf16[2,512,512]{2,1,0:T(8,128)(2,1)S(1)}) custom-call(s32[1]{0:T(128)} %bitcast.micro, s32[2]{0:T(128)S(1)} %copy-done.1, bf16[256,512]{1,0:T(8,128)(2,1)S(1)} %get-tuple-element.157.ga, bf16[2,256,256]{2,1,0:T(8,128)(2,1)S(1)} %copy-done.3, ...), custom_call_target="tpu_custom_call" | custom-call | tf_op jit(solution)/shard_map/slots/pallas_call | solution.py:40
  44.1 1.7 %collective-permute-done.13.from_left = bf16[128,512]{1,0:T(8,128)(2,1)S(1)} collective-permute-done((bf16[128,512]{1,0:T(8,128)(2,1)S(1)}, bf16[128,512]{1,0:T(8,128)(2,1)S(1)}, u32[]{:S(2)}, u32[]{:S(2)}) %collective-permute-start.13) | collective-permute-done | bytes 131104 | tf_op jit(solution)/shard_map/ppermute | solution.py:289
  45.8 0.5 last.1
  46.3 0.1 collective-permute-start.15
  46.4 2.6 %collective-permute-done.15 = bf16[2,512,512]{2,1,0:T(8,128)(2,1)S(1)} collective-permute-done((bf16[2,512,512]{2,1,0:T(8,128)(2,1)S(1)}, bf16[2,512,512]{2,1,0:T(8,128)(2,1)S(1)}, u32[]{:S(2)}, u32[]{:S(2)}) %collective-permute-start.15) | collective-permute-done | bytes 1048608 | tf_op jit(solution)/shard_map/ppermute | solution.py:425
  49.0 0.3 add_convert_fusion
  49.4 21.8 %all_to_all.10 = bf16[16,64,512]{2,1,0:T(8,128)(2,1)S(1)} all-to-all(bf16[16,64,512]{2,1,0:T(8,128)(2,1)S(1)} %bitcast.12), channel_id=1, replica_groups=mesh['segment'=2,'x'=4,'z'=8,'rep'=4] {'x','rep'}, dimensions={0} | all-to-all | bytes 2097152 | tf_op jit(solution)/shard_map/all_to_all | solution.py:428
  71.1 0.1 reduce_sum.12
  71.3 8.4 %collective-permute-start.16 = (bf16[64,512]{1,0:T(8,128)(2,1)S(1)}, bf16[64,512]{1,0:T(8,128)(2,1)S(1)}, u32[]{:S(2)}, u32[]{:S(2)}) collective-permute-start(bf16[64,512]{1,0:T(8,128)(2,1)S(1)} %reduce_sum.12), channel_id=1, source_target_pairs={{0,28},{4,24},{8,20},{12,16},{16,12},{20,8},{24,4},{28,0},{1,29},{... | collective-permute-start | bytes 196616 | tf_op jit(solution)/shard_map/ppermute | solution.py:332
  79.7 2.4 %collective-permute-done.16 = bf16[64,512]{1,0:T(8,128)(2,1)S(1)} collective-permute-done((bf16[64,512]{1,0:T(8,128)(2,1)S(1)}, bf16[64,512]{1,0:T(8,128)(2,1)S(1)}, u32[]{:S(2)}, u32[]{:S(2)}) %collective-permute-start.16) | collective-permute-done | bytes 65568 | tf_op jit(solution)/shard_map/ppermute | solution.py:332
  82.1 0.1 collective-permute-start.19
  82.2 4.8 %collective-permute-start.18 = (bf16[64,512]{1,0:T(8,128)(2,1)S(1)}, bf16[64,512]{1,0:T(8,128)(2,1)S(1)}, u32[]{:S(2)}, u32[]{:S(2)}) collective-permute-start(bf16[64,512]{1,0:T(8,128)(2,1)S(1)} %add_convert_fusion.2), channel_id=1, source_target_pairs={{0,8},{4,12},{8,0},{12,4},{16,24},{20,28},{24,16},{28,20},{1,9},{5... | collective-permute-start | bytes 196616 | tf_op jit(solution)/shard_map/ppermute | solution.py:335
  86.9 0.9 collective-permute-done.19
  87.8 2.1 %collective-permute-done.18 = bf16[64,512]{1,0:T(8,128)(2,1)S(1)} collective-permute-done((bf16[64,512]{1,0:T(8,128)(2,1)S(1)}, bf16[64,512]{1,0:T(8,128)(2,1)S(1)}, u32[]{:S(2)}, u32[]{:S(2)}) %collective-permute-start.18) | collective-permute-done | bytes 65568 | tf_op jit(solution)/shard_map/ppermute | solution.py:335
  90.0 1.3 %collective-permute-done.17 = bf16[64,512]{1,0:T(8,128)(2,1)S(1)} collective-permute-done((bf16[64,512]{1,0:T(8,128)(2,1)S(1)}, bf16[64,512]{1,0:T(8,128)(2,1)S(1)}, u32[]{:S(2)}, u32[]{:S(2)}) %collective-permute-start.17) | collective-permute-done | bytes 65568 | tf_op jit(solution)/shard_map/ppermute | solution.py:335
  91.2 0.1 broadcast_in_dim.10
  91.3 17.7 %all_to_all.11 = bf16[16,64,512]{2,1,0:T(8,128)(2,1)S(1)} all-to-all(bf16[16,64,512]{2,1,0:T(8,128)(2,1)S(1)} %broadcast_in_dim.10), channel_id=1, replica_groups=mesh['segment'=2,'x'=4,'z'=8,'rep'=4] {'x','rep'}, dimensions={0} | all-to-all | bytes 2097152 | tf_op jit(solution)/shard_map/all_to_all | solution.py:430
  109.0 1.6 %bitcast_convert_fusion = f32[2,512,512]{2,1,0:T(8,128)} fusion(bf16[2,512,512]{2,1,0:T(8,128)(2,1)S(1)} %bitcast.13), kind=kLoop, calls=%fused_computation.1 | loop fusion | flops 524288 | bytes 3145728 | tf_op jit(solution)/shard_map/convert_element_type | solution.py:433
  (13 shorter events, 0.1 us)
Async XLA Ops:
  0.0 6.0 %copy-start = (bf16[2,512,512]{2,1,0:T(8,128)(2,1)S(1)}, bf16[2,512,512]{2,1,0:T(8,128)(2,1)}, u32[]{:S(2)}) copy-start(bf16[2,512,512]{2,1,0:T(8,128)(2,1)} %weights.2) | copy-start | bytes 3145732
  1.3 4.8 %collective-permute-start.4 = (bf16[2,512,512]{2,1,0:T(8,128)(2,1)}, bf16[2,512,512]{2,1,0:T(8,128)(2,1)S(1)}, u32[]{:S(2)}, u32[]{:S(2)}) collective-permute-start(bf16[2,512,512]{2,1,0:T(8,128)(2,1)} %weights.2), channel_id=1, source_target_pairs={{0,128},{128,0},{1,129},{129,1},{2,130},{130,2},{3,131},{131,3},{4... | collective-permute-start | bytes 3145736 | tf_op jit(solution)/shard_map/ppermute | solution.py:366
  1.4 6.0 %collective-permute-start.5 = (bf16[128,512]{1,0:T(8,128)(2,1)S(1)}, bf16[128,512]{1,0:T(8,128)(2,1)S(1)}, u32[]{:S(2)}, u32[]{:S(2)}) collective-permute-start(bf16[128,512]{1,0:T(8,128)(2,1)S(1)} %get-tuple-element.132), channel_id=1, source_target_pairs={{0,4},{4,8},{8,12},{12,16},{16,20},{20,24},{24,28},{28,32},{32,36}... | collective-permute-start | bytes 393224 | tf_op jit(solution)/shard_map/ppermute | solution.py:289
  3.4 5.7 %collective-permute-start.6 = (bf16[128,512]{1,0:T(8,128)(2,1)S(1)}, bf16[128,512]{1,0:T(8,128)(2,1)S(1)}, u32[]{:S(2)}, u32[]{:S(2)}) collective-permute-start(bf16[128,512]{1,0:T(8,128)(2,1)S(1)} %get-tuple-element.125), channel_id=1, source_target_pairs={{4,0},{8,4},{12,8},{16,12},{20,16},{24,20},{28,24},{32,28},{36,32}... | collective-permute-start | bytes 393224 | tf_op jit(solution)/shard_map/ppermute | solution.py:289
  6.0 8.5 %copy-start.1 = (s32[2]{0:T(128)S(1)}, s32[2]{0:T(128)}, u32[]{:S(2)}) copy-start(s32[2]{0:T(128)} %layers.2) | copy-start | bytes 28
  6.4 20.4 %copy-start.2 = (bf16[2,256,256]{2,1,0:T(8,128)(2,1)}, bf16[2,256,256]{2,1,0:T(8,128)(2,1)S(1)}, u32[]{:S(2)}) copy-start(bf16[2,256,256]{2,1,0:T(8,128)(2,1)S(1)} %get-tuple-element.136.own) | copy-start | bytes 786436
  9.8 8.2 %collective-permute-start.7 = (bf16[128,512]{1,0:T(8,128)(2,1)S(1)}, bf16[128,512]{1,0:T(8,128)(2,1)S(1)}, u32[]{:S(2)}, u32[]{:S(2)}) collective-permute-start(bf16[128,512]{1,0:T(8,128)(2,1)S(1)} %get-tuple-element.139), channel_id=1, source_target_pairs={{0,4},{4,8},{8,12},{12,16},{16,20},{20,24},{24,28},{28,32},{32,36}... | collective-permute-start | bytes 393224 | tf_op jit(solution)/shard_map/ppermute | solution.py:289
  13.0 5.9 %collective-permute-start.8 = (bf16[128,512]{1,0:T(8,128)(2,1)S(1)}, bf16[128,512]{1,0:T(8,128)(2,1)S(1)}, u32[]{:S(2)}, u32[]{:S(2)}) collective-permute-start(bf16[128,512]{1,0:T(8,128)(2,1)S(1)} %get-tuple-element.140), channel_id=1, source_target_pairs={{4,0},{8,4},{12,8},{16,12},{20,16},{24,20},{28,24},{32,28},{36,32}... | collective-permute-start | bytes 393224 | tf_op jit(solution)/shard_map/ppermute | solution.py:289
  19.6 7.2 %collective-permute-start.9 = (bf16[128,512]{1,0:T(8,128)(2,1)S(1)}, bf16[128,512]{1,0:T(8,128)(2,1)S(1)}, u32[]{:S(2)}, u32[]{:S(2)}) collective-permute-start(bf16[128,512]{1,0:T(8,128)(2,1)S(1)} %get-tuple-element.145), channel_id=1, source_target_pairs={{0,4},{4,8},{8,12},{12,16},{16,20},{20,24},{24,28},{28,32},{32,36}... | collective-permute-start | bytes 393224 | tf_op jit(solution)/shard_map/ppermute | solution.py:289
  21.7 5.1 %collective-permute-start.10 = (bf16[128,512]{1,0:T(8,128)(2,1)S(1)}, bf16[128,512]{1,0:T(8,128)(2,1)S(1)}, u32[]{:S(2)}, u32[]{:S(2)}) collective-permute-start(bf16[128,512]{1,0:T(8,128)(2,1)S(1)} %get-tuple-element.146), channel_id=1, source_target_pairs={{4,0},{8,4},{12,8},{16,12},{20,16},{24,20},{28,24},{32,28},{36,32}... | collective-permute-start | bytes 393224 | tf_op jit(solution)/shard_map/ppermute | solution.py:289
  28.3 14.6 %copy-start.3 = (bf16[2,256,256]{2,1,0:T(8,128)(2,1)S(1)}, bf16[2,256,256]{2,1,0:T(8,128)(2,1)}, u32[]{:S(2)}) copy-start(bf16[2,256,256]{2,1,0:T(8,128)(2,1)} %copy-done.2) | copy-start | bytes 786436
  28.3 8.4 %collective-permute-start.11 = (bf16[128,512]{1,0:T(8,128)(2,1)S(1)}, bf16[128,512]{1,0:T(8,128)(2,1)S(1)}, u32[]{:S(2)}, u32[]{:S(2)}) collective-permute-start(bf16[128,512]{1,0:T(8,128)(2,1)S(1)} %get-tuple-element.154), channel_id=1, source_target_pairs={{0,4},{4,8},{8,12},{12,16},{16,20},{20,24},{24,28},{28,32},{32,36}... | collective-permute-start | bytes 393224 | tf_op jit(solution)/shard_map/ppermute | solution.py:289
  29.8 6.9 %collective-permute-start.12 = (bf16[128,512]{1,0:T(8,128)(2,1)S(1)}, bf16[128,512]{1,0:T(8,128)(2,1)S(1)}, u32[]{:S(2)}, u32[]{:S(2)}) collective-permute-start(bf16[128,512]{1,0:T(8,128)(2,1)S(1)} %get-tuple-element.155), channel_id=1, source_target_pairs={{4,0},{8,4},{12,8},{16,12},{20,16},{24,20},{28,24},{32,28},{36,32}... | collective-permute-start | bytes 393224 | tf_op jit(solution)/shard_map/ppermute | solution.py:289
  37.4 8.4 %collective-permute-start.13 = (bf16[128,512]{1,0:T(8,128)(2,1)S(1)}, bf16[128,512]{1,0:T(8,128)(2,1)S(1)}, u32[]{:S(2)}, u32[]{:S(2)}) collective-permute-start(bf16[128,512]{1,0:T(8,128)(2,1)S(1)} %get-tuple-element.163), channel_id=1, source_target_pairs={{0,4},{4,8},{8,12},{12,16},{16,20},{20,24},{24,28},{28,32},{32,36}... | collective-permute-start | bytes 393224 | tf_op jit(solution)/shard_map/ppermute | solution.py:289
  37.5 8.3 %collective-permute-start.14 = (bf16[128,512]{1,0:T(8,128)(2,1)S(1)}, bf16[128,512]{1,0:T(8,128)(2,1)S(1)}, u32[]{:S(2)}, u32[]{:S(2)}) collective-permute-start(bf16[128,512]{1,0:T(8,128)(2,1)S(1)} %get-tuple-element.164), channel_id=1, source_target_pairs={{4,0},{8,4},{12,8},{16,12},{20,16},{24,20},{28,24},{32,28},{36,32}... | collective-permute-start | bytes 393224 | tf_op jit(solution)/shard_map/ppermute | solution.py:289
  46.3 2.7 %collective-permute-start.15 = (bf16[2,512,512]{2,1,0:T(8,128)(2,1)S(1)}, bf16[2,512,512]{2,1,0:T(8,128)(2,1)S(1)}, u32[]{:S(2)}, u32[]{:S(2)}) collective-permute-start(bf16[2,512,512]{2,1,0:T(8,128)(2,1)S(1)} %get-tuple-element.170), channel_id=1, source_target_pairs={{0,128},{128,0},{1,129},{129,1},{2,130},{130,2},{3,131},{131,3},{4... | collective-permute-start | bytes 3145736 | tf_op jit(solution)/shard_map/ppermute | solution.py:425
  71.3 10.8 %collective-permute-start.16 = (bf16[64,512]{1,0:T(8,128)(2,1)S(1)}, bf16[64,512]{1,0:T(8,128)(2,1)S(1)}, u32[]{:S(2)}, u32[]{:S(2)}) collective-permute-start(bf16[64,512]{1,0:T(8,128)(2,1)S(1)} %reduce_sum.12), channel_id=1, source_target_pairs={{0,28},{4,24},{8,20},{12,16},{16,12},{20,8},{24,4},{28,0},{1,29},{... | collective-permute-start | bytes 196616 | tf_op jit(solution)/shard_map/ppermute | solution.py:332
  82.1 5.8 %collective-permute-start.19 = (bf16[64,512]{1,0:T(8,128)(2,1)S(1)}, bf16[64,512]{1,0:T(8,128)(2,1)S(1)}, u32[]{:S(2)}, u32[]{:S(2)}) collective-permute-start(bf16[64,512]{1,0:T(8,128)(2,1)S(1)} %add_convert_fusion.2), channel_id=1, source_target_pairs={{0,12},{4,8},{8,4},{12,0},{16,28},{20,24},{24,20},{28,16},{1,13},{... | collective-permute-start | bytes 196616 | tf_op jit(solution)/shard_map/ppermute | solution.py:335
  82.2 7.8 %collective-permute-start.18 = (bf16[64,512]{1,0:T(8,128)(2,1)S(1)}, bf16[64,512]{1,0:T(8,128)(2,1)S(1)}, u32[]{:S(2)}, u32[]{:S(2)}) collective-permute-start(bf16[64,512]{1,0:T(8,128)(2,1)S(1)} %add_convert_fusion.2), channel_id=1, source_target_pairs={{0,8},{4,12},{8,0},{12,4},{16,24},{20,28},{24,16},{28,20},{1,9},{5... | collective-permute-start | bytes 196616 | tf_op jit(solution)/shard_map/ppermute | solution.py:335
  86.9 4.3 %collective-permute-start.17 = (bf16[64,512]{1,0:T(8,128)(2,1)S(1)}, bf16[64,512]{1,0:T(8,128)(2,1)S(1)}, u32[]{:S(2)}, u32[]{:S(2)}) collective-permute-start(bf16[64,512]{1,0:T(8,128)(2,1)S(1)} %add_convert_fusion.2), channel_id=1, source_target_pairs={{0,4},{4,0},{8,12},{12,8},{16,20},{20,16},{24,28},{28,24},{1,5},{5... | collective-permute-start | bytes 196616 | tf_op jit(solution)/shard_map/ppermute | solution.py:335
where the time goes:
time: 111 us
  blocking collectives  39.5 us (36%)
  starting transfers between devices  35.6 us (32%)
  waiting for transfers between devices  19.4 us (17%)
  Pallas kernels  10.9 us (10%)
  other arithmetic  2.13 us (2%)
  local copies, waits for them, and re-layouts  1.43 us (1%)
  between operations  1.42 us (1%)
    ppermute x10, starting transfers between devices, exchange(): return (lax.ppermute(to_right, DOM, up), lax.ppermute(to_left, DOM, down))  22.2 us
    all_to_all x1, blocking collectives, shards(): lax.all_to_all(part.reshape(plane, -1, FEAT), PLANE, 0, 0, tiled=True)  21.8 us
    all_to_all x1, blocking collectives, shards(): lax.all_to_all(jnp.broadcast_to(piece[None], (plane,) + piece.shape), PLA...  17.7 us
    pallas_call x11, Pallas kernels, call(): pl.pallas_call(kernel, out_shape=outs, in_specs=smem + held, scratch_shap...  10.9 us
    ppermute x10, waiting for transfers between devices, exchange(): return (lax.ppermute(to_right, DOM, up), lax.ppermute(to_left, DOM, down))  10.1 us
    ppermute x1, starting transfers between devices, along_z(): got = lax.ppermute(piece, 'z', [(i, depth - 1 - i) for i in range(depth)])  8.42 us
    ppermute x3, starting transfers between devices, along_z(): lax.ppermute(piece, 'z', [(i, i ^ k) for i in range(depth)]).astype(F32)  4.85 us
    ppermute x3, waiting for transfers between devices, along_z(): lax.ppermute(piece, 'z', [(i, i ^ k) for i in range(depth)]).astype(F32)  4.26 us
  transfers between devices with their start and end apart: 16, of which 12 were waited for; matrix products, arithmetic and copies ran while one was open for 1% of the time, Pallas kernels for 5%

commit v1 on v0

--- a/solution.py
+++ b/solution.py
@@ -270,6 +270,21 @@
     @pl.when(micro[0] == 1)
     def _():
         given[0] = grad
+
+
+PIECES = 8
+
+
+def widen_kernel(source, out, wide, sems):
+    rows = source.shape[0] // PIECES
+    copies = []
+    for i in range(PIECES):
+        span = pl.ds(i * rows, rows)
+        wide[span, :] = source[span, :].astype(F32)
+        copies.append(pltpu.make_async_copy(wide.at[span, :], out.at[span, :], sems.at[i]))
+        copies[-1].start()
+    for copy in copies:
+        copy.wait()
 
 
 HALF = spec((BLOCK, FEAT), BF)
@@ -430,7 +445,17 @@
     whole = lax.all_to_all(
         jnp.broadcast_to(piece[None], (plane,) + piece.shape), PLANE, 0, 0, tiled=True
     )
-    return whole.reshape(2, FEAT, FEAT).astype(F32)
+    flat = whole.reshape(2 * FEAT, FEAT)
+    wide = pl.pallas_call(
+        widen_kernel,
+        out_shape=spec(flat.shape, F32),
+        in_specs=[pl.BlockSpec(memory_space=pltpu.VMEM)],
+        out_specs=pl.BlockSpec(memory_space=pltpu.HBM),
+        scratch_shapes=[pltpu.VMEM(flat.shape, F32), pltpu.SemaphoreType.DMA((PIECES,))],
+        compiler_params=pltpu.CompilerParams(vmem_limit_bytes=12 * 1024 * 1024),
+        name="widen",
+    )(flat)
+    return wide.reshape(2, FEAT, FEAT)
 
 
 def solution(mesh):

time: 111 us -> 111 us (level)
  other arithmetic: 2.13 us -> 0.52 us
  Pallas kernels: 10.9 us -> 12.3 us
    convert_element_type x1 -> x0, other arithmetic: 1.61 us -> none  [shards(): return whole.reshape(2, FEAT, FEAT).astype(F32)]
    pallas_call x0 -> x1, Pallas kernels: none -> 1.39 us  [shards(): pl.pallas_call(widen_kernel, out_shape=spec(flat.shape, F32), in_specs=[p...]
where the time goes in v1:
time: 111 us
  blocking collectives  39.5 us (36%)
  starting transfers between devices  35.6 us (32%)
  waiting for transfers between devices  19.4 us (17%)
  Pallas kernels  12.3 us (11%)
  between operations  1.6 us (1%)
  local copies, waits for them, and re-layouts  1.43 us (1%)
    ppermute x10, starting transfers between devices, exchange(): return (lax.ppermute(to_right, DOM, up), lax.ppermute(to_left, DOM, down))  22.2 us
    all_to_all x1, blocking collectives, shards(): lax.all_to_all(part.reshape(plane, -1, FEAT), PLANE, 0, 0, tiled=True)  21.8 us
    all_to_all x1, blocking collectives, shards(): lax.all_to_all(jnp.broadcast_to(piece[None], (plane,) + piece.shape), PLA...  17.7 us
    pallas_call x11, Pallas kernels, call(): pl.pallas_call(kernel, out_shape=outs, in_specs=smem + held, scratch_shap...  10.9 us
    ppermute x10, waiting for transfers between devices, exchange(): return (lax.ppermute(to_right, DOM, up), lax.ppermute(to_left, DOM, down))  10.1 us
    ppermute x1, starting transfers between devices, along_z(): got = lax.ppermute(piece, 'z', [(i, depth - 1 - i) for i in range(depth)])  8.42 us
    ppermute x3, starting transfers between devices, along_z(): lax.ppermute(piece, 'z', [(i, i ^ k) for i in range(depth)]).astype(F32)  4.85 us
    ppermute x3, waiting for transfers between devices, along_z(): lax.ppermute(piece, 'z', [(i, i ^ k) for i in range(depth)]).astype(F32)  4.26 us
  transfers between devices with their start and end apart: 16, of which 12 were waited for; matrix products, arithmetic and copies ran while one was open for 1% of the time, Pallas kernels for 5%

profile of v1, /device:TPU:32, one launch (start us, length us, event | category | flops | bytes accessed | tf_op | source)
XLA Modules:
  0.0 110.6 jit_solution(3585702894861819155)
XLA Ops:
  0.0 1.3 %first.1 = (bf16[128,512]{1,0:T(8,128)(2,1)S(1)}, bf16[128,512]{1,0:T(8,128)(2,1)S(1)}, bf16[6,128,128]{2,1,0:T(8,128)(2,1)S(1)}, bf16[2,128,512]{2,1,0:T(8,128)...) custom-call(s32[1]{0:T(128)} %bitcast.micro, s32[2,2]{1,0:T(2,128)} %bitcast.15, s32[2,6]{1,0:T(2,128)} %bitcast.16, ...), custom_call_target="tpu_custom_call" | custom-call | tf_op jit(solution)/shard_map/first/pallas_call | solution.py:40
  1.3 0.1 collective-permute-start.4
  1.4 2.0 %collective-permute-start.5 = (bf16[128,512]{1,0:T(8,128)(2,1)S(1)}, bf16[128,512]{1,0:T(8,128)(2,1)S(1)}, u32[]{:S(2)}, u32[]{:S(2)}) collective-permute-start(bf16[128,512]{1,0:T(8,128)(2,1)S(1)} %get-tuple-element.132), channel_id=1, source_target_pairs={{0,4},{4,8},{8,12},{12,16},{16,20},{20,24},{24,28},{28,32},{32,36}... | collective-permute-start | bytes 393224 | tf_op jit(solution)/shard_map/ppermute | solution.py:304
  3.4 0.1 collective-permute-start.6
  3.5 1.3 %fusion = (s32[1]{0:T(128)}, s32[1]{0:T(128)}) fusion(s32[2]{0:T(128)} %layers.2), kind=kLoop, calls=%fused_computation.3 | loop fusion | bytes 16 | tf_op jit(solution)/shard_map/slice | solution.py:379
  6.0 0.0 copy-start.1
  6.0 0.4 prep.1
  6.4 0.0 copy-start.2
  6.4 0.9 collective-permute-done.5.from_left
  7.4 1.7 %collective-permute-done.6.from_right = bf16[128,512]{1,0:T(8,128)(2,1)S(1)} collective-permute-done((bf16[128,512]{1,0:T(8,128)(2,1)S(1)}, bf16[128,512]{1,0:T(8,128)(2,1)S(1)}, u32[]{:S(2)}, u32[]{:S(2)}) %collective-permute-start.6) | collective-permute-done | bytes 131104 | tf_op jit(solution)/shard_map/ppermute | solution.py:304
  9.1 0.7 forward1.1
  9.8 3.2 %collective-permute-start.7 = (bf16[128,512]{1,0:T(8,128)(2,1)S(1)}, bf16[128,512]{1,0:T(8,128)(2,1)S(1)}, u32[]{:S(2)}, u32[]{:S(2)}) collective-permute-start(bf16[128,512]{1,0:T(8,128)(2,1)S(1)} %get-tuple-element.139), channel_id=1, source_target_pairs={{0,4},{4,8},{8,12},{12,16},{16,20},{20,24},{24,28},{28,32},{32,36}... | collective-permute-start | bytes 393224 | tf_op jit(solution)/shard_map/ppermute | solution.py:304
  13.0 1.6 %collective-permute-start.8 = (bf16[128,512]{1,0:T(8,128)(2,1)S(1)}, bf16[128,512]{1,0:T(8,128)(2,1)S(1)}, u32[]{:S(2)}, u32[]{:S(2)}) collective-permute-start(bf16[128,512]{1,0:T(8,128)(2,1)S(1)} %get-tuple-element.140), channel_id=1, source_target_pairs={{4,0},{8,4},{12,8},{16,12},{20,16},{24,20},{28,24},{32,28},{36,32}... | collective-permute-start | bytes 393224 | tf_op jit(solution)/shard_map/ppermute | solution.py:304
  14.6 1.4 %rest1.1 = (f32[256,512]{1,0:T(8,128)S(1)}, f32[256,512]{1,0:T(8,128)S(1)}, bf16[512,512]{1,0:T(8,128)(2,1)S(1)}) custom-call(s32[1]{0:T(128)} %bitcast.micro, s32[2]{0:T(128)S(1)} %copy-done.1, bf16[256,512]{1,0:T(8,128)(2,1)S(1)} %get-tuple-element.135.out, bf16[2,128,512]{2,1,0:T(8,128)(2,1)S(1)} %get-tuple-element.129.feats, ...), custom_call_target="tpu_custom_call" | custom-call | tf_op jit(solution)/shard_map/rest1/pallas_call | solution.py:40
  16.0 2.0 %collective-permute-done.7.from_left = bf16[128,512]{1,0:T(8,128)(2,1)S(1)} collective-permute-done((bf16[128,512]{1,0:T(8,128)(2,1)S(1)}, bf16[128,512]{1,0:T(8,128)(2,1)S(1)}, u32[]{:S(2)}, u32[]{:S(2)}) %collective-permute-start.7) | collective-permute-done | bytes 131104 | tf_op jit(solution)/shard_map/ppermute | solution.py:304
  18.0 0.9 collective-permute-done.8.from_right
  18.9 0.7 forward2.1
  19.6 2.1 %collective-permute-start.9 = (bf16[128,512]{1,0:T(8,128)(2,1)S(1)}, bf16[128,512]{1,0:T(8,128)(2,1)S(1)}, u32[]{:S(2)}, u32[]{:S(2)}) collective-permute-start(bf16[128,512]{1,0:T(8,128)(2,1)S(1)} %get-tuple-element.145), channel_id=1, source_target_pairs={{0,4},{4,8},{8,12},{12,16},{16,20},{20,24},{24,28},{28,32},{32,36}... | collective-permute-start | bytes 393224 | tf_op jit(solution)/shard_map/ppermute | solution.py:304
  21.7 2.2 %collective-permute-start.10 = (bf16[128,512]{1,0:T(8,128)(2,1)S(1)}, bf16[128,512]{1,0:T(8,128)(2,1)S(1)}, u32[]{:S(2)}, u32[]{:S(2)}) collective-permute-start(bf16[128,512]{1,0:T(8,128)(2,1)S(1)} %get-tuple-element.146), channel_id=1, source_target_pairs={{4,0},{8,4},{12,8},{16,12},{20,16},{24,20},{28,24},{32,28},{36,32}... | collective-permute-start | bytes 393224 | tf_op jit(solution)/shard_map/ppermute | solution.py:304
  23.9 1.4 %rest2.1 = (f32[256,512]{1,0:T(8,128)S(1)}, f32[256,512]{1,0:T(8,128)S(1)}, bf16[512,512]{1,0:T(8,128)(2,1)S(1)}, bf16[512,512]{1,0:T(8,128)(2,1)S(1)}) custom-call(s32[1]{0:T(128)} %bitcast.micro, s32[2]{0:T(128)S(1)} %copy-done.1, bf16[256,512]{1,0:T(8,128)(2,1)S(1)} %get-tuple-element.142.out, bf16[2,128,512]{2,1,0:T(8,128)(2,1)S(1)} %get-tuple-element.129.feats, ...), custom_call_target="tpu_custom_call" | custom-call | tf_op jit(solution)/shard_map/rest2/pallas_call | solution.py:40
  25.4 1.4 %collective-permute-done.9 = bf16[128,512]{1,0:T(8,128)(2,1)S(1)} collective-permute-done((bf16[128,512]{1,0:T(8,128)(2,1)S(1)}, bf16[128,512]{1,0:T(8,128)(2,1)S(1)}, u32[]{:S(2)}, u32[]{:S(2)}) %collective-permute-start.9) | collective-permute-done | bytes 131104 | tf_op jit(solution)/shard_map/ppermute | solution.py:304
  26.8 1.5 %conditional.1 = (bf16[512,512]{1,0:T(8,128)(2,1)S(1)}, bf16[256,512]{1,0:T(8,128)(2,1)S(1)}, bf16[256,512]{1,0:T(8,128)(2,1)S(1)}, bf16[256,512]{1,0:T(8,128)(2...) conditional(s32[]{:T(128)} %bitcast.6, (f32[256,512]{1,0:T(8,128)S(1)}, ...), branch_computations={%region_0.0_spmd, %region_1.0_spmd} | conditional | bytes 2097360 | solution.py:420
  26.8 1.3 %top3.1 = (bf16[256,512]{1,0:T(8,128)(2,1)S(1)}, bf16[256,512]{1,0:T(8,128)(2,1)S(1)}, bf16[256,512]{1,0:T(8,128)(2,1)S(1)}, bf16[128,512]{1,0:T(8,128)(2,1)S(1)...) custom-call(f32[256,512]{1,0:T(8,128)S(1)} %get-tuple-element.37.base, ...), custom_call_target="tpu_custom_call" | custom-call | tf_op jit(solution)/shard_map/cond/branch_0_fun/top3/pallas_call | solution.py:40
  28.3 1.5 %collective-permute-start.11 = (bf16[128,512]{1,0:T(8,128)(2,1)S(1)}, bf16[128,512]{1,0:T(8,128)(2,1)S(1)}, u32[]{:S(2)}, u32[]{:S(2)}) collective-permute-start(bf16[128,512]{1,0:T(8,128)(2,1)S(1)} %get-tuple-element.154), channel_id=1, source_target_pairs={{0,4},{4,8},{8,12},{12,16},{16,20},{20,24},{24,28},{28,32},{32,36}... | collective-permute-start | bytes 393224 | tf_op jit(solution)/shard_map/ppermute | solution.py:304
  29.8 4.0 %collective-permute-start.12 = (bf16[128,512]{1,0:T(8,128)(2,1)S(1)}, bf16[128,512]{1,0:T(8,128)(2,1)S(1)}, u32[]{:S(2)}, u32[]{:S(2)}) collective-permute-start(bf16[128,512]{1,0:T(8,128)(2,1)S(1)} %get-tuple-element.155), channel_id=1, source_target_pairs={{4,0},{8,4},{12,8},{16,12},{20,16},{24,20},{28,24},{32,28},{36,32}... | collective-permute-start | bytes 393224 | tf_op jit(solution)/shard_map/ppermute | solution.py:304
  33.8 1.4 %backrest3.1 = (f32[256,512]{1,0:T(8,128)S(1)}, bf16[512,512]{1,0:T(8,128)(2,1)S(1)}) custom-call(bf16[256,512]{1,0:T(8,128)(2,1)S(1)} %get-tuple-element.150.ga, bf16[2,256,256]{2,1,0:T(8,128)(2,1)} %copy-done.2, bf16[256,512]{1,0:T(8,128)(2,1)S(1)} %get-tuple-element.151.mix, bf16[256,512]{1,0:T(8,128)(2,1)S(1)} %get-tuple-element.152.gz_round), custom_call_target="tpu_custom_call" | custom-call | tf_op jit(solution)/shard_map/backrest3/pallas_call | solution.py:40
  35.2 1.4 %collective-permute-done.11.from_left = bf16[128,512]{1,0:T(8,128)(2,1)S(1)} collective-permute-done((bf16[128,512]{1,0:T(8,128)(2,1)S(1)}, bf16[128,512]{1,0:T(8,128)(2,1)S(1)}, u32[]{:S(2)}, u32[]{:S(2)}) %collective-permute-start.11) | collective-permute-done | bytes 131104 | tf_op jit(solution)/shard_map/ppermute | solution.py:304
  36.7 0.7 back2.1
  37.4 0.1 collective-permute-start.13
  37.5 5.4 %collective-permute-start.14 = (bf16[128,512]{1,0:T(8,128)(2,1)S(1)}, bf16[128,512]{1,0:T(8,128)(2,1)S(1)}, u32[]{:S(2)}, u32[]{:S(2)}) collective-permute-start(bf16[128,512]{1,0:T(8,128)(2,1)S(1)} %get-tuple-element.164), channel_id=1, source_target_pairs={{4,0},{8,4},{12,8},{16,12},{20,16},{24,20},{28,24},{32,28},{36,32}... | collective-permute-start | bytes 393224 | tf_op jit(solution)/shard_map/ppermute | solution.py:304
  42.9 1.2 %slots.1 = (f32[256,512]{1,0:T(8,128)S(1)}, bf16[2,512,512]{2,1,0:T(8,128)(2,1)S(1)}, bf16[2,512,512]{2,1,0:T(8,128)(2,1)S(1)}) custom-call(s32[1]{0:T(128)} %bitcast.micro, s32[2]{0:T(128)S(1)} %copy-done.1, bf16[256,512]{1,0:T(8,128)(2,1)S(1)} %get-tuple-element.157.ga, bf16[2,256,256]{2,1,0:T(8,128)(2,1)S(1)} %copy-done.3, ...), custom_call_target="tpu_custom_call" | custom-call | tf_op jit(solution)/shard_map/slots/pallas_call | solution.py:40
  44.1 1.7 %collective-permute-done.13.from_left = bf16[128,512]{1,0:T(8,128)(2,1)S(1)} collective-permute-done((bf16[128,512]{1,0:T(8,128)(2,1)S(1)}, bf16[128,512]{1,0:T(8,128)(2,1)S(1)}, u32[]{:S(2)}, u32[]{:S(2)}) %collective-permute-start.13) | collective-permute-done | bytes 131104 | tf_op jit(solution)/shard_map/ppermute | solution.py:304
  45.8 0.5 last.1
  46.3 0.1 collective-permute-start.15
  46.4 2.6 %collective-permute-done.15 = bf16[2,512,512]{2,1,0:T(8,128)(2,1)S(1)} collective-permute-done((bf16[2,512,512]{2,1,0:T(8,128)(2,1)S(1)}, bf16[2,512,512]{2,1,0:T(8,128)(2,1)S(1)}, u32[]{:S(2)}, u32[]{:S(2)}) %collective-permute-start.15) | collective-permute-done | bytes 1048608 | tf_op jit(solution)/shard_map/ppermute | solution.py:440
  49.0 0.3 add_convert_fusion
  49.4 21.8 %all_to_all.10 = bf16[16,64,512]{2,1,0:T(8,128)(2,1)S(1)} all-to-all(bf16[16,64,512]{2,1,0:T(8,128)(2,1)S(1)} %bitcast.11), channel_id=1, replica_groups=mesh['segment'=2,'x'=4,'z'=8,'rep'=4] {'x','rep'}, dimensions={0} | all-to-all | bytes 2097152 | tf_op jit(solution)/shard_map/all_to_all | solution.py:443
  71.1 0.1 reduce_sum.12
  71.3 8.4 %collective-permute-start.16 = (bf16[64,512]{1,0:T(8,128)(2,1)S(1)}, bf16[64,512]{1,0:T(8,128)(2,1)S(1)}, u32[]{:S(2)}, u32[]{:S(2)}) collective-permute-start(bf16[64,512]{1,0:T(8,128)(2,1)S(1)} %reduce_sum.12), channel_id=1, source_target_pairs={{0,28},{4,24},{8,20},{12,16},{16,12},{20,8},{24,4},{28,0},{1,29},{... | collective-permute-start | bytes 196616 | tf_op jit(solution)/shard_map/ppermute | solution.py:347
  79.7 2.4 %collective-permute-done.16 = bf16[64,512]{1,0:T(8,128)(2,1)S(1)} collective-permute-done((bf16[64,512]{1,0:T(8,128)(2,1)S(1)}, bf16[64,512]{1,0:T(8,128)(2,1)S(1)}, u32[]{:S(2)}, u32[]{:S(2)}) %collective-permute-start.16) | collective-permute-done | bytes 65568 | tf_op jit(solution)/shard_map/ppermute | solution.py:347
  82.1 0.1 collective-permute-start.19
  82.2 4.8 %collective-permute-start.18 = (bf16[64,512]{1,0:T(8,128)(2,1)S(1)}, bf16[64,512]{1,0:T(8,128)(2,1)S(1)}, u32[]{:S(2)}, u32[]{:S(2)}) collective-permute-start(bf16[64,512]{1,0:T(8,128)(2,1)S(1)} %add_convert_fusion.2), channel_id=1, source_target_pairs={{0,8},{4,12},{8,0},{12,4},{16,24},{20,28},{24,16},{28,20},{1,9},{5... | collective-permute-start | bytes 196616 | tf_op jit(solution)/shard_map/ppermute | solution.py:350
  86.9 0.9 collective-permute-done.19
  87.8 2.1 %collective-permute-done.18 = bf16[64,512]{1,0:T(8,128)(2,1)S(1)} collective-permute-done((bf16[64,512]{1,0:T(8,128)(2,1)S(1)}, bf16[64,512]{1,0:T(8,128)(2,1)S(1)}, u32[]{:S(2)}, u32[]{:S(2)}) %collective-permute-start.18) | collective-permute-done | bytes 65568 | tf_op jit(solution)/shard_map/ppermute | solution.py:350
  90.0 1.3 %collective-permute-done.17 = bf16[64,512]{1,0:T(8,128)(2,1)S(1)} collective-permute-done((bf16[64,512]{1,0:T(8,128)(2,1)S(1)}, bf16[64,512]{1,0:T(8,128)(2,1)S(1)}, u32[]{:S(2)}, u32[]{:S(2)}) %collective-permute-start.17) | collective-permute-done | bytes 65568 | tf_op jit(solution)/shard_map/ppermute | solution.py:350
  91.2 0.1 broadcast_in_dim.10
  91.3 17.7 %all_to_all.11 = bf16[16,64,512]{2,1,0:T(8,128)(2,1)S(1)} all-to-all(bf16[16,64,512]{2,1,0:T(8,128)(2,1)S(1)} %broadcast_in_dim.10), channel_id=1, replica_groups=mesh['segment'=2,'x'=4,'z'=8,'rep'=4] {'x','rep'}, dimensions={0} | all-to-all | bytes 2097152 | tf_op jit(solution)/shard_map/all_to_all | solution.py:445
  109.0 1.4 %widen.1 = f32[1024,512]{1,0:T(8,128)} custom-call(bf16[1024,512]{1,0:T(8,128)(2,1)S(1)} %bitcast.10), custom_call_target="tpu_custom_call" | custom-call | tf_op jit(solution)/shard_map/widen/pallas_call | solution.py:449
  (13 shorter events, 0.1 us)
Async XLA Ops:
  0.0 6.0 %copy-start = (bf16[2,512,512]{2,1,0:T(8,128)(2,1)S(1)}, bf16[2,512,512]{2,1,0:T(8,128)(2,1)}, u32[]{:S(2)}) copy-start(bf16[2,512,512]{2,1,0:T(8,128)(2,1)} %weights.2) | copy-start | bytes 3145732
  1.3 4.8 %collective-permute-start.4 = (bf16[2,512,512]{2,1,0:T(8,128)(2,1)}, bf16[2,512,512]{2,1,0:T(8,128)(2,1)S(1)}, u32[]{:S(2)}, u32[]{:S(2)}) collective-permute-start(bf16[2,512,512]{2,1,0:T(8,128)(2,1)} %weights.2), channel_id=1, source_target_pairs={{0,128},{128,0},{1,129},{129,1},{2,130},{130,2},{3,131},{131,3},{4... | collective-permute-start | bytes 3145736 | tf_op jit(solution)/shard_map/ppermute | solution.py:381
  1.4 6.0 %collective-permute-start.5 = (bf16[128,512]{1,0:T(8,128)(2,1)S(1)}, bf16[128,512]{1,0:T(8,128)(2,1)S(1)}, u32[]{:S(2)}, u32[]{:S(2)}) collective-permute-start(bf16[128,512]{1,0:T(8,128)(2,1)S(1)} %get-tuple-element.132), channel_id=1, source_target_pairs={{0,4},{4,8},{8,12},{12,16},{16,20},{20,24},{24,28},{28,32},{32,36}... | collective-permute-start | bytes 393224 | tf_op jit(solution)/shard_map/ppermute | solution.py:304
  3.4 5.7 %collective-permute-start.6 = (bf16[128,512]{1,0:T(8,128)(2,1)S(1)}, bf16[128,512]{1,0:T(8,128)(2,1)S(1)}, u32[]{:S(2)}, u32[]{:S(2)}) collective-permute-start(bf16[128,512]{1,0:T(8,128)(2,1)S(1)} %get-tuple-element.125), channel_id=1, source_target_pairs={{4,0},{8,4},{12,8},{16,12},{20,16},{24,20},{28,24},{32,28},{36,32}... | collective-permute-start | bytes 393224 | tf_op jit(solution)/shard_map/ppermute | solution.py:304
  6.0 8.5 %copy-start.1 = (s32[2]{0:T(128)S(1)}, s32[2]{0:T(128)}, u32[]{:S(2)}) copy-start(s32[2]{0:T(128)} %layers.2) | copy-start | bytes 28
  6.4 20.4 %copy-start.2 = (bf16[2,256,256]{2,1,0:T(8,128)(2,1)}, bf16[2,256,256]{2,1,0:T(8,128)(2,1)S(1)}, u32[]{:S(2)}) copy-start(bf16[2,256,256]{2,1,0:T(8,128)(2,1)S(1)} %get-tuple-element.136.own) | copy-start | bytes 786436
  9.8 8.2 %collective-permute-start.7 = (bf16[128,512]{1,0:T(8,128)(2,1)S(1)}, bf16[128,512]{1,0:T(8,128)(2,1)S(1)}, u32[]{:S(2)}, u32[]{:S(2)}) collective-permute-start(bf16[128,512]{1,0:T(8,128)(2,1)S(1)} %get-tuple-element.139), channel_id=1, source_target_pairs={{0,4},{4,8},{8,12},{12,16},{16,20},{20,24},{24,28},{28,32},{32,36}... | collective-permute-start | bytes 393224 | tf_op jit(solution)/shard_map/ppermute | solution.py:304
  13.0 5.9 %collective-permute-start.8 = (bf16[128,512]{1,0:T(8,128)(2,1)S(1)}, bf16[128,512]{1,0:T(8,128)(2,1)S(1)}, u32[]{:S(2)}, u32[]{:S(2)}) collective-permute-start(bf16[128,512]{1,0:T(8,128)(2,1)S(1)} %get-tuple-element.140), channel_id=1, source_target_pairs={{4,0},{8,4},{12,8},{16,12},{20,16},{24,20},{28,24},{32,28},{36,32}... | collective-permute-start | bytes 393224 | tf_op jit(solution)/shard_map/ppermute | solution.py:304
  19.6 7.2 %collective-permute-start.9 = (bf16[128,512]{1,0:T(8,128)(2,1)S(1)}, bf16[128,512]{1,0:T(8,128)(2,1)S(1)}, u32[]{:S(2)}, u32[]{:S(2)}) collective-permute-start(bf16[128,512]{1,0:T(8,128)(2,1)S(1)} %get-tuple-element.145), channel_id=1, source_target_pairs={{0,4},{4,8},{8,12},{12,16},{16,20},{20,24},{24,28},{28,32},{32,36}... | collective-permute-start | bytes 393224 | tf_op jit(solution)/shard_map/ppermute | solution.py:304
  21.7 5.1 %collective-permute-start.10 = (bf16[128,512]{1,0:T(8,128)(2,1)S(1)}, bf16[128,512]{1,0:T(8,128)(2,1)S(1)}, u32[]{:S(2)}, u32[]{:S(2)}) collective-permute-start(bf16[128,512]{1,0:T(8,128)(2,1)S(1)} %get-tuple-element.146), channel_id=1, source_target_pairs={{4,0},{8,4},{12,8},{16,12},{20,16},{24,20},{28,24},{32,28},{36,32}... | collective-permute-start | bytes 393224 | tf_op jit(solution)/shard_map/ppermute | solution.py:304
  28.3 14.6 %copy-start.3 = (bf16[2,256,256]{2,1,0:T(8,128)(2,1)S(1)}, bf16[2,256,256]{2,1,0:T(8,128)(2,1)}, u32[]{:S(2)}) copy-start(bf16[2,256,256]{2,1,0:T(8,128)(2,1)} %copy-done.2) | copy-start | bytes 786436
  28.3 8.4 %collective-permute-start.11 = (bf16[128,512]{1,0:T(8,128)(2,1)S(1)}, bf16[128,512]{1,0:T(8,128)(2,1)S(1)}, u32[]{:S(2)}, u32[]{:S(2)}) collective-permute-start(bf16[128,512]{1,0:T(8,128)(2,1)S(1)} %get-tuple-element.154), channel_id=1, source_target_pairs={{0,4},{4,8},{8,12},{12,16},{16,20},{20,24},{24,28},{28,32},{32,36}... | collective-permute-start | bytes 393224 | tf_op jit(solution)/shard_map/ppermute | solution.py:304
  29.8 6.9 %collective-permute-start.12 = (bf16[128,512]{1,0:T(8,128)(2,1)S(1)}, bf16[128,512]{1,0:T(8,128)(2,1)S(1)}, u32[]{:S(2)}, u32[]{:S(2)}) collective-permute-start(bf16[128,512]{1,0:T(8,128)(2,1)S(1)} %get-tuple-element.155), channel_id=1, source_target_pairs={{4,0},{8,4},{12,8},{16,12},{20,16},{24,20},{28,24},{32,28},{36,32}... | collective-permute-start | bytes 393224 | tf_op jit(solution)/shard_map/ppermute | solution.py:304
  37.4 8.4 %collective-permute-start.13 = (bf16[128,512]{1,0:T(8,128)(2,1)S(1)}, bf16[128,512]{1,0:T(8,128)(2,1)S(1)}, u32[]{:S(2)}, u32[]{:S(2)}) collective-permute-start(bf16[128,512]{1,0:T(8,128)(2,1)S(1)} %get-tuple-element.163), channel_id=1, source_target_pairs={{0,4},{4,8},{8,12},{12,16},{16,20},{20,24},{24,28},{28,32},{32,36}... | collective-permute-start | bytes 393224 | tf_op jit(solution)/shard_map/ppermute | solution.py:304
  37.5 8.3 %collective-permute-start.14 = (bf16[128,512]{1,0:T(8,128)(2,1)S(1)}, bf16[128,512]{1,0:T(8,128)(2,1)S(1)}, u32[]{:S(2)}, u32[]{:S(2)}) collective-permute-start(bf16[128,512]{1,0:T(8,128)(2,1)S(1)} %get-tuple-element.164), channel_id=1, source_target_pairs={{4,0},{8,4},{12,8},{16,12},{20,16},{24,20},{28,24},{32,28},{36,32}... | collective-permute-start | bytes 393224 | tf_op jit(solution)/shard_map/ppermute | solution.py:304
  46.3 2.7 %collective-permute-start.15 = (bf16[2,512,512]{2,1,0:T(8,128)(2,1)S(1)}, bf16[2,512,512]{2,1,0:T(8,128)(2,1)S(1)}, u32[]{:S(2)}, u32[]{:S(2)}) collective-permute-start(bf16[2,512,512]{2,1,0:T(8,128)(2,1)S(1)} %get-tuple-element.170), channel_id=1, source_target_pairs={{0,128},{128,0},{1,129},{129,1},{2,130},{130,2},{3,131},{131,3},{4... | collective-permute-start | bytes 3145736 | tf_op jit(solution)/shard_map/ppermute | solution.py:440
  71.3 10.8 %collective-permute-start.16 = (bf16[64,512]{1,0:T(8,128)(2,1)S(1)}, bf16[64,512]{1,0:T(8,128)(2,1)S(1)}, u32[]{:S(2)}, u32[]{:S(2)}) collective-permute-start(bf16[64,512]{1,0:T(8,128)(2,1)S(1)} %reduce_sum.12), channel_id=1, source_target_pairs={{0,28},{4,24},{8,20},{12,16},{16,12},{20,8},{24,4},{28,0},{1,29},{... | collective-permute-start | bytes 196616 | tf_op jit(solution)/shard_map/ppermute | solution.py:347
  82.1 5.8 %collective-permute-start.19 = (bf16[64,512]{1,0:T(8,128)(2,1)S(1)}, bf16[64,512]{1,0:T(8,128)(2,1)S(1)}, u32[]{:S(2)}, u32[]{:S(2)}) collective-permute-start(bf16[64,512]{1,0:T(8,128)(2,1)S(1)} %add_convert_fusion.2), channel_id=1, source_target_pairs={{0,12},{4,8},{8,4},{12,0},{16,28},{20,24},{24,20},{28,16},{1,13},{... | collective-permute-start | bytes 196616 | tf_op jit(solution)/shard_map/ppermute | solution.py:350
  82.2 7.8 %collective-permute-start.18 = (bf16[64,512]{1,0:T(8,128)(2,1)S(1)}, bf16[64,512]{1,0:T(8,128)(2,1)S(1)}, u32[]{:S(2)}, u32[]{:S(2)}) collective-permute-start(bf16[64,512]{1,0:T(8,128)(2,1)S(1)} %add_convert_fusion.2), channel_id=1, source_target_pairs={{0,8},{4,12},{8,0},{12,4},{16,24},{20,28},{24,16},{28,20},{1,9},{5... | collective-permute-start | bytes 196616 | tf_op jit(solution)/shard_map/ppermute | solution.py:350
  86.9 4.3 %collective-permute-start.17 = (bf16[64,512]{1,0:T(8,128)(2,1)S(1)}, bf16[64,512]{1,0:T(8,128)(2,1)S(1)}, u32[]{:S(2)}, u32[]{:S(2)}) collective-permute-start(bf16[64,512]{1,0:T(8,128)(2,1)S(1)} %add_convert_fusion.2), channel_id=1, source_target_pairs={{0,4},{4,0},{8,12},{12,8},{16,20},{20,16},{24,28},{28,24},{1,5},{5... | collective-permute-start | bytes 196616 | tf_op jit(solution)/shard_map/ppermute | solution.py:350
